TPU v7x, 512 devices: a whole 4x4x16 slice. The times are simulated.
512 devices in a mesh: dp: 64 (over z_lo, x, y), tensor: 8 (over z_hi, core).
Axes of the slice: x: 4, y: 4, z: 16 (z_hi: 4, z_lo: 4; z = z_hi * 4 + z_lo), core: 2. Of those that a mesh axis runs over, the one named last changes fastest.
Arguments:
- activations: bfloat16 [64, 256, 8192], P('dp', None, 'tensor'), may hold values from -6 to 6
- output_grads: bfloat16 [64, 256, 8192], P('dp', None, 'tensor'), may hold values from -0.375 to 0.375
- projection: bfloat16 [8192, 128], P('tensor'), may hold values from -0.0625 to 0.0625
- token_counts: int32 [64], P('dp'), may hold values from 64 to 256, as said below
- hessian_inverse: bfloat16 [4096, 4096], P('dp', 'tensor')
- queries: bfloat16 [1024, 4096], P('dp', 'tensor'), may hold values from -0.09375 to 0.09375
Outputs:
- scores: float32 [64, 1024], P('dp', 'tensor')
Inputs may be any that keep to these rules, and one draw needn't show every extreme that they name: `token_counts`: in every draw some example uses all 256 positions and some uses exactly 64.
All inputs are finite; a program needn't handle non-finite values.
Results may differ from a plain program's by a relative error of at most 0.004.
Values may be sent and summed in bfloat16 or wider, within the bound.
A program may use at most 64 MiB of HBM per device.

v0:
```python
import jax
import jax.numpy as jnp
from jax import lax
from jax.sharding import PartitionSpec as P


def masked_rows(flat_acts, flat_grads, projection, token_counts, row_count, length):
    width = projection.shape[1] // 2
    inputs_side = jnp.dot(flat_acts, projection[:, :width], preferred_element_type=jnp.float32)
    output_side = jnp.dot(flat_grads, projection[:, width:], preferred_element_type=jnp.float32)
    places = jnp.arange(row_count, dtype=jnp.int32)
    owners = places // length
    member = owners[:, None] == jnp.arange(token_counts.shape[0], dtype=jnp.int32)[None, :]
    limits = jnp.sum(jnp.where(member, token_counts[None, :], 0), axis=1)
    inside = (places % length < limits).astype(jnp.float32)
    return jnp.concatenate([inputs_side, output_side], axis=1) * inside[:, None]


def on_device(activations, output_grads, projection, token_counts, hessian_inverse, queries):
    examples_here, length, feature_part = activations.shape
    width = projection.shape[1] // 2
    total_rows = examples_here * length
    flat_acts = activations.reshape(total_rows, feature_part)
    flat_grads = output_grads.reshape(total_rows, feature_part)
    summed = lax.psum(
        masked_rows(flat_acts, flat_grads, projection, token_counts, total_rows, length), "tensor"
    )
    shaped = summed.reshape(examples_here, length, 2 * width)
    outer = jnp.einsum(
        "eta,etb->eab", shaped[:, :, width:], shaped[:, :, :width], precision=lax.Precision.HIGHEST
    )
    factor_sum = outer.reshape(examples_here, width * width)
    factor = factor_sum.astype(jnp.bfloat16)
    blocks = lax.all_to_all(factor, "dp", split_axis=1, concat_axis=0, tiled=True)
    precond_total = lax.psum_scatter(
        jnp.dot(blocks, hessian_inverse, preferred_element_type=jnp.float32),
        "dp",
        scatter_dimension=0,
        tiled=True,
    )
    preconditioned = precond_total.astype(jnp.bfloat16)
    contract = (((1,), (1,)), ((), ()))
    partial_scores = lax.dot_general(
        preconditioned,
        lax.all_gather(queries, "dp", axis=0, tiled=True),
        contract,
        preferred_element_type=jnp.float32,
    )
    return lax.psum_scatter(partial_scores, "tensor", scatter_dimension=1, tiled=True)


def solution(mesh):
    placed = (
        P("dp", None, "tensor"),
        P("dp", None, "tensor"),
        P("tensor", None),
        P("dp"),
        P("dp", "tensor"),
        P("dp", "tensor"),
    )
    return jax.shard_map(
        on_device, mesh=mesh, in_specs=placed, out_specs=P("dp", "tensor"), check_vma=False
    )
```

profile of v0, /device:TPU:1, one launch (start us, length us, event | category | flops | bytes accessed | tf_op | source)
XLA Modules:
  0.0 551.7 jit_solution(2973602964388223871)
XLA Ops:
  7.4 0.0 copy-start
  7.4 0.0 copy-start.2
  7.4 0.0 all-reduce.4.cloned.1.call-start
  8.1 0.3 copy-done
  8.4 0.0 copy-start.1
  8.4 1.3 fusion.3
  9.7 0.0 copy-done.2
  9.7 0.0 copy-done.1
  9.8 0.4 fusion.1
  10.2 0.7 fusion.7
  10.9 0.0 all-reduce.4.cloned.1.call-update
  10.9 0.0 all-gather.2.cloned.1.call-start
  10.9 0.5 all-gather.2.cloned.1.call-update
  11.5 101.4 %all-reduce.4.cloned.1.call-done = f32[1,256,128]{1,2,0:T(8,128)} async-done(((f32[1,256,128]{1,2,0:T(8,128)}), f32[1,256,128]{1,2,0:T(8,128)}) %all-reduce.4.cloned.1.call-update) | async-done | bytes 131088 | tf_op jit(solution)/shard_map/psum | solution.py:25
  112.9 1.1 fusion
  114.0 0.0 copy-start.3
  114.0 0.6 copy.8
  114.6 10.1 %all-to-all-start = ((bf16[1,64,64]{2,0,1:T(2,128)(2,1)}), bf16[1,64,64]{2,0,1:T(2,128)(2,1)S(1)}, u32[]{:S(2)}, u32[]{:S(2)}) async-start(bf16[1,64,64]{2,0,1:T(2,128)(2,1)} %copy.8), calls=%async_computation | async-start | bytes 65536 | tf_op jit(solution)/shard_map/all_to_all | solution.py:34
  124.7 0.0 reduce-scatter.4.cloned.1.call-start
  124.8 1.3 dynamic-slice
  126.0 7.7 %all-to-all-done = bf16[1,64,64]{2,0,1:T(2,128)(2,1)S(1)} async-done(((bf16[1,64,64]{2,0,1:T(2,128)(2,1)}), bf16[1,64,64]{2,0,1:T(2,128)(2,1)S(1)}, u32[]{:S(2)}, u32[]{:S(2)}) %all-to-all-start) | async-done | bytes 8224 | tf_op jit(solution)/shard_map/all_to_all | solution.py:34
  133.7 0.0 copy-done.3
  133.7 0.1 fusion.8
  133.8 309.3 %all-reduce.5 = bf16[64,512]{1,0:T(8,128)(2,1)S(1)} all-reduce(f32[64,512]{1,0:T(8,128)S(1)} %fusion.8), channel_id=2, replica_groups=mesh['dp'=64,'tensor'=8] {'dp'}, use_global_device_ids=true, to_apply=%region_1.2.clone | all-reduce | flops 32768 | bytes 196608
  443.2 0.0 all-gather.2.cloned.1.call-done
  443.2 3.1 convolution_bitcast_fusion
  446.2 0.0 reduce-scatter.4.cloned.1.call-update
  446.3 96.5 %reduce-scatter.4.cloned.1.call-done = f32[128,1]{1,0:T(8,128)} async-done(((f32[1024,1]{1,0:T(8,128)}), f32[128,1]{1,0:T(8,128)}) %reduce-scatter.4.cloned.1.call-update) | async-done | bytes 528
  542.8 1.4 copy.10
  (1 shorter events, 0.0 us)
Async XLA Ops:
  7.4 1.1 copy-start
  7.4 2.4 copy-start.2
  7.4 105.5 %all-reduce.4.cloned.1.call-start = ((), (), s32[]{:S(2)}) async-start(), calls=%async_computation.2 | async-start | bytes 262144 | tf_op jit(solution)/shard_map/psum | solution.py:25
  8.4 1.3 copy-start.1
  10.9 432.3 %all-gather.2.cloned.1.call-start = ((), (), s32[]{:S(2)}) async-start(), calls=%async_computation.3 | async-start | bytes 1064960 | tf_op jit(solution)/shard_map/all_gather | solution.py:45
  114.0 19.7 %copy-start.3 = (bf16[64,512]{1,0:T(8,128)(2,1)S(1)}, bf16[64,512]{1,0:T(8,128)(2,1)}, u32[]{:S(2)}) copy-start(bf16[64,512]{1,0:T(8,128)(2,1)} %param.10) | copy-start | bytes 196612
  114.6 19.1 %all-to-all-start = ((bf16[1,64,64]{2,0,1:T(2,128)(2,1)}), bf16[1,64,64]{2,0,1:T(2,128)(2,1)S(1)}, u32[]{:S(2)}, u32[]{:S(2)}) async-start(bf16[1,64,64]{2,0,1:T(2,128)(2,1)} %copy.8), calls=%async_computation | async-start | bytes 65536 | tf_op jit(solution)/shard_map/all_to_all | solution.py:34
  124.7 418.1 %reduce-scatter.4.cloned.1.call-start = ((), (), s32[]{:S(2)}) async-start(), calls=%async_computation.4 | async-start | bytes 589824
Sparse Core Ops, SparseCore 0:
  11.1 101.7 all-reduce.3
  446.4 96.3 reduce-scatter.3
Sparse Core Ops, SparseCore 1:
  13.6 311.2 all-gather.1
where the time goes:
time: 552 us
  blocking collectives  309 us (56%)
  waiting for transfers between devices  206 us (37%)
  between operations  15.6 us (3%)
  starting transfers between devices  10.1 us (2%)
  matrix products  6.01 us (1%)
    unnamed x1, blocking collectives  309 us
    psum x1, waiting for transfers between devices, on_device(): lax.psum(masked_rows(flat_acts, flat_grads, projection, token_counts, tot...  101 us
    unnamed x4, waiting for transfers between devices  97.1 us
  transfers between devices with their start and end apart: 4, of which 3 were waited for; matrix products, arithmetic and copies ran while one was open for 1% of the time, Pallas kernels for 0%

commit v1 on v0

v1 whole, which is shorter than its diff:
```python
import jax
import jax.numpy as jnp
from jax import lax
from jax.experimental import pallas as pl
from jax.experimental.pallas import tpu as pltpu
from jax.sharding import PartitionSpec as P

MESH = pl.DeviceIdType.MESH
NEAR = 16
RUNS = 4
RANK = 64
HALF = 128
PLANE = sorted(range(1, NEAR), key=lambda k: -(min(k // 4, 4 - k // 4) + min(k % 4, 4 - k % 4)))


def attribute(
    acts_hbm, grads_hbm, proj_hbm, counts_hbm, hess_hbm, query_hbm, out,
    acts, grads, proj, counts, rows, pair, wire, wires, partial, partner, factor, factors,
    hess, query, product, others, summed, blocks, gathered, part, parts,
    load_sem, send_sem, recv_sem, block_sem, known,
):
    d, s = lax.axis_index("dp"), lax.axis_index("tensor")
    run, plane = d // NEAR, lax.rem(d, NEAR)
    px, py = plane // 4, lax.rem(plane, 4)
    group, core = s // 2, lax.rem(s, 2)
    z = group * RUNS + run

    def at(run_, plane_, group_, core_):
        return (run_ * NEAR + plane_, group_ * 2 + core_)

    def ring(k):
        there = lax.rem(z + k + 16, 16)
        return at(lax.rem(there, RUNS), plane, there // RUNS, core)

    def beside(k):
        return at(run, lax.rem(px + k // 4, 4) * 4 + lax.rem(py + k % 4, 4), group, core)

    def along(k):
        return at(lax.rem(run + k, RUNS), plane, group, core)

    def across(k):
        return at(run, plane, lax.rem(group + k, RUNS), core)

    sibling = at(run, plane, group, 1 - core)

    def send(src, dst, k, device):
        pltpu.make_async_remote_copy(
            src, dst, send_sem.at[k], recv_sem.at[k], device_id=device, device_id_type=MESH
        ).start()

    def arrived(ref, k):
        pltpu.make_async_copy(ref, ref, recv_sem.at[k]).wait()

    def left(ref, k):
        pltpu.make_async_copy(ref, ref, send_sem.at[k]).wait()

    barrier = pltpu.get_barrier_semaphore()
    greeted = [beside(k) for k in PLANE] + [ring(k) for k in (4, -4, 3, -3, 2, -2, 1, -1)] + [sibling]
    for device in greeted:
        pl.semaphore_signal(barrier, inc=1, device_id=device, device_id_type=MESH)
    loads = [
        pltpu.make_async_copy(query_hbm, query.at[plane], load_sem.at[0]),
        pltpu.make_async_copy(hess_hbm, hess.at[run], load_sem.at[1]),
        pltpu.make_async_copy(proj_hbm, proj, load_sem.at[2]),
        pltpu.make_async_copy(acts_hbm, acts, load_sem.at[3]),
        pltpu.make_async_copy(grads_hbm, grads, load_sem.at[4]),
        pltpu.make_async_copy(counts_hbm, counts, load_sem.at[5]),
    ]
    for load in loads:
        load.start()

    for load in loads[2:]:
        load.wait()
    lane = lax.broadcasted_iota(jnp.int32, (2 * HALF, 2 * RANK), 1)
    position = lax.broadcasted_iota(jnp.int32, (2 * HALF, 2 * RANK), 0)
    inputs_side = jnp.dot(acts[0], proj[...], preferred_element_type=jnp.float32)
    output_side = jnp.dot(grads[0], proj[...], preferred_element_type=jnp.float32)
    projected = jnp.where(lane < RANK, inputs_side, output_side)
    projected = jnp.where(position < counts[0], projected, 0.0)
    rows[0] = projected[:HALF]
    rows[1] = projected[HALF:]
    for load in loads[:2]:
        load.wait()

    pl.semaphore_wait(barrier, len(greeted))
    for k in (4, -4):
        pl.semaphore_signal(known, inc=1, device_id=ring(k), device_id_type=MESH)
    send(rows.at[1 - core], pair, 0, sibling)
    for k in PLANE:
        send(query.at[plane], query.at[plane], 1, beside(k))
    for k in (2, 1, 3):
        send(hess.at[run], hess.at[run], 2, along(k))
    arrived(pair, 0)
    chip = rows[core] + pair[...]
    wire[...] = chip.astype(jnp.bfloat16)
    pl.semaphore_wait(known, 2)
    for k in (2, 1, 3):
        send(wire, wires.at[k - 1], 3, across(k))

    arrived(query.at[pl.ds(0, NEAR - 1)], 1)
    arrived(hess.at[pl.ds(0, RUNS - 1)], 2)
    contract = (((1,), (1,)), ((), ()))
    rows_of_hess = hess[...].reshape(RUNS * RANK, 512)

    def times(which):
        some = query[pl.ds(which * 8, 8)].reshape(HALF, 512)
        result = lax.dot_general(rows_of_hess, some, contract, preferred_element_type=jnp.float32)
        return result.reshape(RUNS, RANK, HALF)

    product[...] = times(1 - core)
    send(product, others, 4, sibling)
    own = times(core)
    arrived(others, 4)
    summed[...] = own + others[...]
    for k in range(RUNS):
        stays = jnp.logical_and(group == run, run == k)

        @pl.when(jnp.logical_not(stays))
        def _():
            pltpu.make_async_remote_copy(
                summed.at[k], blocks.at[group], block_sem.at[k], recv_sem.at[5],
                device_id=at(k, plane, run, core), device_id_type=MESH,
            ).start()

        @pl.when(stays)
        def _():
            pltpu.make_async_copy(summed.at[k], blocks.at[group], recv_sem.at[5]).start()

    arrived(wires, 3)
    whole = chip + (
        wires[0].astype(jnp.float32) + wires[1].astype(jnp.float32) + wires[2].astype(jnp.float32)
    )
    outer = lax.dot_general(
        whole, whole, (((0,), (0,)), ((), ())),
        precision=lax.Precision.HIGHEST, preferred_element_type=jnp.float32,
    )
    partial[...] = outer[RANK:]
    send(partial, partner, 6, sibling)
    arrived(partner, 6)
    rounded = (partial[...] + partner[...]).astype(jnp.bfloat16)
    to = lax.broadcasted_iota(jnp.int32, (NEAR * 8, RANK), 0)
    come = lax.broadcasted_iota(jnp.int32, (NEAR * 8, RANK), 1)
    to_run, to_plane = lax.rem(to, 8), lax.div(to, 8)
    chosen = jnp.logical_and(to_run < RUNS, come == to_run * NEAR + to_plane)
    order = jnp.where(chosen, 1.0, 0.0).astype(jnp.bfloat16)
    ordered = jnp.dot(order, rounded, preferred_element_type=jnp.float32)
    factor[...] = ordered.reshape(NEAR, 8, 2 * RANK)
    for k in PLANE:
        there = lax.rem(px + k // 4, 4) * 4 + lax.rem(py + k % 4, 4)
        send(factor.at[there], factors.at[plane], 7, beside(k))
    factors[plane] = factor[plane]

    arrived(blocks, 5)
    gathered[run] = (blocks[0] + blocks[1] + (blocks[2] + blocks[3])).astype(jnp.bfloat16)
    for k in (2, 1, 3):
        send(gathered.at[run], gathered.at[run], 8, along(k))
    arrived(factors.at[pl.ds(0, NEAR - 1)], 7)
    left_side = factors[...].reshape(NEAR * 8, 2 * RANK)[:, :RANK].astype(jnp.bfloat16)
    which = lax.rem(lax.broadcasted_iota(jnp.int32, (NEAR * 8, HALF), 0), 8)
    arrived(gathered.at[pl.ds(0, RUNS - 1)], 8)
    scores = jnp.zeros((NEAR * 8, HALF), jnp.float32)
    for k in range(RUNS):
        term = jnp.dot(left_side, gathered[k], preferred_element_type=jnp.float32)
        scores += jnp.where(which == k, term, 0.0)
    part[...] = scores.reshape(NEAR, 8, HALF)
    for k in PLANE:
        there = lax.rem(px + k // 4, 4) * 4 + lax.rem(py + k % 4, 4)
        send(part.at[there], parts.at[plane], 9, beside(k))
    parts[plane] = part[plane]

    left(pair, 0)
    left(query.at[pl.ds(0, NEAR - 1)], 1)
    left(hess.at[pl.ds(0, RUNS - 1)], 2)
    left(wires, 3)
    left(others, 4)
    left(partner, 6)
    left(factors.at[pl.ds(0, NEAR - 1)], 7)
    left(gathered.at[pl.ds(0, RUNS - 1)], 8)
    for k in range(RUNS):
        @pl.when(jnp.logical_not(jnp.logical_and(group == run, run == k)))
        def _():
            pltpu.make_async_copy(summed.at[k], summed.at[k], block_sem.at[k]).wait()
    arrived(parts.at[pl.ds(0, NEAR - 1)], 9)
    total = jnp.sum(parts[...], axis=0)
    out[...] = jnp.sum(total, axis=0, keepdims=True)
    left(parts.at[pl.ds(0, NEAR - 1)], 9)


def on_device(activations, output_grads, projection, token_counts, hessian_inverse, queries):
    anywhere = pl.BlockSpec(memory_space=pltpu.HBM)
    bf16, f32 = jnp.bfloat16, jnp.float32
    scratch = [
        pltpu.VMEM((1, 256, 1024), bf16),
        pltpu.VMEM((1, 256, 1024), bf16),
        pltpu.VMEM((1024, 128), bf16),
        pltpu.SMEM((1,), jnp.int32),
        pltpu.VMEM((2, HALF, 128), f32),
        pltpu.VMEM((HALF, 128), f32),
        pltpu.VMEM((HALF, 128), bf16),
        pltpu.VMEM((RUNS - 1, HALF, 128), bf16),
        pltpu.VMEM((RANK, 128), f32),
        pltpu.VMEM((RANK, 128), f32),
        pltpu.VMEM((NEAR, 8, 128), f32),
        pltpu.VMEM((NEAR, 8, 128), f32),
        pltpu.VMEM((RUNS, RANK, 512), bf16),
        pltpu.VMEM((NEAR, 16, 512), bf16),
        pltpu.VMEM((RUNS, RANK, HALF), f32),
        pltpu.VMEM((RUNS, RANK, HALF), f32),
        pltpu.VMEM((RUNS, RANK, HALF), f32),
        pltpu.VMEM((RUNS, RANK, HALF), f32),
        pltpu.VMEM((RUNS, RANK, HALF), bf16),
        pltpu.VMEM((NEAR, 8, HALF), f32),
        pltpu.VMEM((NEAR, 8, HALF), f32),
        pltpu.SemaphoreType.DMA((6,)),
        pltpu.SemaphoreType.DMA((10,)),
        pltpu.SemaphoreType.DMA((10,)),
        pltpu.SemaphoreType.DMA((RUNS,)),
        pltpu.SemaphoreType.REGULAR,
    ]
    return pl.pallas_call(
        attribute,
        out_shape=jax.ShapeDtypeStruct((1, HALF), f32),
        in_specs=[anywhere] * 6,
        out_specs=pl.BlockSpec(memory_space=pltpu.VMEM),
        scratch_shapes=scratch,
        compiler_params=pltpu.CompilerParams(
            collective_id=0, has_side_effects=True, vmem_limit_bytes=60 << 20
        ),
        cost_estimate=pl.CostEstimate(flops=200_000_000, bytes_accessed=1_500_000, transcendentals=0),
        name="attribute",
    )(activations, output_grads, projection, token_counts, hessian_inverse, queries)


def solution(mesh):
    placed = (
        P("dp", None, "tensor"),
        P("dp", None, "tensor"),
        P("tensor", None),
        P("dp"),
        P("dp", "tensor"),
        P("dp", "tensor"),
    )
    return jax.shard_map(
        on_device, mesh=mesh, in_specs=placed, out_specs=P("dp", "tensor"), check_vma=False
    )
```

time: 552 us -> 49.8 us (0.09)
  blocking collectives: 309 us -> 0 us
  waiting for transfers between devices: 206 us -> 0 us
  Pallas kernels: 0 us -> 47.8 us
  between operations: 15.6 us -> 0.66 us
  starting transfers between devices: 10.1 us -> 0 us
  matrix products: 6.01 us -> 0 us
    unnamed x1 -> x0, blocking collectives: 309 us -> none
    psum x1 -> x0, waiting for transfers between devices: 101 us -> none  [on_device(): lax.psum(masked_rows(flat_acts, flat_grads, projection, token_counts, tot...]
    unnamed x4 -> x0, waiting for transfers between devices: 97.1 us -> none
    pallas_call x0 -> x1, Pallas kernels: none -> 47.8 us  [on_device(): pl.pallas_call(attribute, out_shape=jax.ShapeDtypeStruct((1, HALF), f32),...]
    all_to_all x1 -> x0, starting transfers between devices: 10.1 us -> none  [on_device(): lax.all_to_all(factor, 'dp', split_axis=1, concat_axis=0, tiled=True)]
    all_to_all x1 -> x0, waiting for transfers between devices: 7.66 us -> none  [on_device(): lax.all_to_all(factor, 'dp', split_axis=1, concat_axis=0, tiled=True)]
  transfers between devices with their start and end apart: 4 -> 0, of which waited for: 3 -> 0; matrix products, arithmetic and copies ran while one was open for 1% -> 0% of each run, Pallas kernels for 0% -> 0%
where the time goes in v1:
time: 49.8 us; the launch traced here: 49.6 us
  Pallas kernels  47.8 us (96%)
  local copies, waits for them, and re-layouts  1.19 us (2%)
  between operations  0.66 us (1%)
    pallas_call x1, Pallas kernels, on_device(): pl.pallas_call(attribute, out_shape=jax.ShapeDtypeStruct((1, HALF), f32),...  47.8 us
    unnamed x1, local copies, waits for them, and re-layouts  1.19 us

profile of v1, /device:TPU:1, one launch (start us, length us, event | category | flops | bytes accessed | tf_op | source)
XLA Modules:
  0.0 49.6 jit_solution(2507524200148493004)
XLA Ops:
  0.7 47.8 %attribute.1 = f32[1,128]{1,0:T(1,128)} custom-call(bf16[1,256,1024]{2,1,0:T(8,128)(2,1)} %acts_hbm.1, bf16[1,256,1024]{2,1,0:T(8,128)(2,1)} %grads_hbm.1, bf16[1024,128]{1,0:T(8,128)(2,1)} %proj_hbm.1, s32[1]{0:T(128)S(6)} %copy.8.counts_hbm, bf16[64,512]{1,0:T(8,128)(2,1)} %hess_hbm.1, bf16[16,512]{1,0:T(8,128)(2,1)} %query_hbm.1), custom_call_target="tpu_custom_call" | custom-call | flops 200000000 | bytes 1500000 | tf_op jit(solution)/shard_map/attribute/pallas_call | solution.py:220
  48.4 1.2 %copy.9 = f32[1,128]{1,0:T(1,128)} copy(f32[1,128]{1,0:T(1,128)} %attribute.1) | data formatting | bytes 1024

commit v2 on v1

--- a/solution.py
+++ b/solution.py
@@ -13,9 +13,19 @@
 PLANE = sorted(range(1, NEAR), key=lambda k: -(min(k // 4, 4 - k // 4) + min(k % 4, 4 - k % 4)))
 
 
+def encode(values):
+    most = jnp.maximum(jnp.max(jnp.abs(values), axis=0, keepdims=True), 1e-30)
+    codes = jnp.round(values * (32000.0 / most)).astype(jnp.int32).astype(jnp.int16)
+    return codes, jnp.broadcast_to(most * (1.0 / 32000.0), (8, 128))
+
+
+def decode(codes, scales):
+    return codes.astype(jnp.int32).astype(jnp.float32) * scales[:1]
+
+
 def attribute(
     acts_hbm, grads_hbm, proj_hbm, counts_hbm, hess_hbm, query_hbm, out,
-    acts, grads, proj, counts, rows, pair, wire, wires, partial, partner, factor, factors,
+    acts, grads, proj, counts, rows, pair, codes, codes_in, scales, scales_in, partial, partner, factor, factors,
     hess, query, product, others, summed, blocks, gathered, part, parts,
     load_sem, send_sem, recv_sem, block_sem, known,
 ):
@@ -92,10 +102,20 @@
         send(hess.at[run], hess.at[run], 2, along(k))
     arrived(pair, 0)
     chip = rows[core] + pair[...]
-    wire[...] = chip.astype(jnp.bfloat16)
-    pl.semaphore_wait(known, 2)
-    for k in (2, 1, 3):
-        send(wire, wires.at[k - 1], 3, across(k))
+    halves = [chip[: HALF // 2], chip[HALF // 2 :]]
+    for step in range(2):
+        for half in range(2):
+            slot = 2 * step + half
+            codes[slot], scales[slot] = encode(halves[half])
+            partner_group = lax.rem(group + 1 + 2 * lax.rem(group + slot // 2 + half, 2), RUNS)
+            device = at(run, plane, partner_group, core)
+            send(codes.at[slot], codes_in.at[slot], 10 + slot, device)
+            send(scales.at[slot], scales_in.at[slot], 14 + slot, device)
+        if step == 0:
+            for half in range(2):
+                arrived(codes.at[half], 10 + half)
+                arrived(scales.at[half], 14 + half)
+                halves[half] = halves[half] + decode(codes_in[half], scales_in[half])
 
     arrived(query.at[pl.ds(0, NEAR - 1)], 1)
     arrived(hess.at[pl.ds(0, RUNS - 1)], 2)
@@ -111,7 +131,8 @@
     send(product, others, 4, sibling)
     own = times(core)
     arrived(others, 4)
-    summed[...] = own + others[...]
+    summed[...] = (own + others[...]).astype(jnp.bfloat16)
+    pl.semaphore_wait(known, 2)
     for k in range(RUNS):
         stays = jnp.logical_and(group == run, run == k)
 
@@ -126,10 +147,11 @@
         def _():
             pltpu.make_async_copy(summed.at[k], blocks.at[group], recv_sem.at[5]).start()
 
-    arrived(wires, 3)
-    whole = chip + (
-        wires[0].astype(jnp.float32) + wires[1].astype(jnp.float32) + wires[2].astype(jnp.float32)
-    )
+    for half in range(2):
+        arrived(codes.at[2 + half], 12 + half)
+        arrived(scales.at[2 + half], 16 + half)
+        halves[half] = halves[half] + decode(codes_in[2 + half], scales_in[2 + half])
+    whole = jnp.concatenate(halves, axis=0)
     outer = lax.dot_general(
         whole, whole, (((0,), (0,)), ((), ())),
         precision=lax.Precision.HIGHEST, preferred_element_type=jnp.float32,
@@ -151,7 +173,8 @@
     factors[plane] = factor[plane]
 
     arrived(blocks, 5)
-    gathered[run] = (blocks[0] + blocks[1] + (blocks[2] + blocks[3])).astype(jnp.bfloat16)
+    b = blocks[...].astype(jnp.float32)
+    gathered[run] = (b[0] + b[1] + (b[2] + b[3])).astype(jnp.bfloat16)
     for k in (2, 1, 3):
         send(gathered.at[run], gathered.at[run], 8, along(k))
     arrived(factors.at[pl.ds(0, NEAR - 1)], 7)
@@ -171,7 +194,9 @@
     left(pair, 0)
     left(query.at[pl.ds(0, NEAR - 1)], 1)
     left(hess.at[pl.ds(0, RUNS - 1)], 2)
-    left(wires, 3)
+    for slot in range(4):
+        left(codes.at[slot], 10 + slot)
+        left(scales.at[slot], 14 + slot)
     left(others, 4)
     left(partner, 6)
     left(factors.at[pl.ds(0, NEAR - 1)], 7)
@@ -196,8 +221,10 @@
         pltpu.SMEM((1,), jnp.int32),
         pltpu.VMEM((2, HALF, 128), f32),
         pltpu.VMEM((HALF, 128), f32),
-        pltpu.VMEM((HALF, 128), bf16),
-        pltpu.VMEM((RUNS - 1, HALF, 128), bf16),
+        pltpu.VMEM((4, HALF // 2, 128), jnp.int16),
+        pltpu.VMEM((4, HALF // 2, 128), jnp.int16),
+        pltpu.VMEM((4, 8, 128), f32),
+        pltpu.VMEM((4, 8, 128), f32),
         pltpu.VMEM((RANK, 128), f32),
         pltpu.VMEM((RANK, 128), f32),
         pltpu.VMEM((NEAR, 8, 128), f32),
@@ -206,14 +233,14 @@
         pltpu.VMEM((NEAR, 16, 512), bf16),
         pltpu.VMEM((RUNS, RANK, HALF), f32),
         pltpu.VMEM((RUNS, RANK, HALF), f32),
-        pltpu.VMEM((RUNS, RANK, HALF), f32),
-        pltpu.VMEM((RUNS, RANK, HALF), f32),
+        pltpu.VMEM((RUNS, RANK, HALF), bf16),
+        pltpu.VMEM((RUNS, RANK, HALF), bf16),
         pltpu.VMEM((RUNS, RANK, HALF), bf16),
         pltpu.VMEM((NEAR, 8, HALF), f32),
         pltpu.VMEM((NEAR, 8, HALF), f32),
         pltpu.SemaphoreType.DMA((6,)),
-        pltpu.SemaphoreType.DMA((10,)),
-        pltpu.SemaphoreType.DMA((10,)),
+        pltpu.SemaphoreType.DMA((18,)),
+        pltpu.SemaphoreType.DMA((18,)),
         pltpu.SemaphoreType.DMA((RUNS,)),
         pltpu.SemaphoreType.REGULAR,
     ]

time: 49.8 us -> 44 us (0.88)
  Pallas kernels: 47.8 us -> 41.8 us
    pallas_call x1, Pallas kernels: 47.8 us -> 41.8 us  [on_device(): pl.pallas_call(attribute, out_shape=jax.ShapeDtypeStruct((1, HALF), f32),...]
where the time goes in v2:
time: 44 us; the launch traced here: 43.7 us
  Pallas kernels  41.8 us (95%)
  local copies, waits for them, and re-layouts  1.19 us (3%)
  between operations  0.66 us (2%)
    pallas_call x1, Pallas kernels, on_device(): pl.pallas_call(attribute, out_shape=jax.ShapeDtypeStruct((1, HALF), f32),...  41.8 us
    unnamed x1, local copies, waits for them, and re-layouts  1.19 us

profile of v2, /device:TPU:1, one launch (start us, length us, event | category | flops | bytes accessed | tf_op | source)
XLA Modules:
  0.0 43.7 jit_solution(15789715998049666894)
XLA Ops:
  0.7 41.8 %attribute.1 = f32[1,128]{1,0:T(1,128)} custom-call(bf16[1,256,1024]{2,1,0:T(8,128)(2,1)} %acts_hbm.1, bf16[1,256,1024]{2,1,0:T(8,128)(2,1)} %grads_hbm.1, bf16[1024,128]{1,0:T(8,128)(2,1)} %proj_hbm.1, s32[1]{0:T(128)S(6)} %copy.8.counts_hbm, bf16[64,512]{1,0:T(8,128)(2,1)} %hess_hbm.1, bf16[16,512]{1,0:T(8,128)(2,1)} %query_hbm.1), custom_call_target="tpu_custom_call" | custom-call | flops 200000000 | bytes 1500000 | tf_op jit(solution)/shard_map/attribute/pallas_call | solution.py:247
  42.5 1.2 %copy.9 = f32[1,128]{1,0:T(1,128)} copy(f32[1,128]{1,0:T(1,128)} %attribute.1) | data formatting | bytes 1024

commit v3 on v2

--- a/solution.py
+++ b/solution.py
@@ -27,20 +27,15 @@
     acts_hbm, grads_hbm, proj_hbm, counts_hbm, hess_hbm, query_hbm, out,
     acts, grads, proj, counts, rows, pair, codes, codes_in, scales, scales_in, partial, partner, factor, factors,
     hess, query, product, others, summed, blocks, gathered, part, parts,
-    load_sem, send_sem, recv_sem, block_sem, known,
+    load_sem, send_sem, recv_sem,
 ):
     d, s = lax.axis_index("dp"), lax.axis_index("tensor")
     run, plane = d // NEAR, lax.rem(d, NEAR)
     px, py = plane // 4, lax.rem(plane, 4)
     group, core = s // 2, lax.rem(s, 2)
-    z = group * RUNS + run
 
     def at(run_, plane_, group_, core_):
         return (run_ * NEAR + plane_, group_ * 2 + core_)
-
-    def ring(k):
-        there = lax.rem(z + k + 16, 16)
-        return at(lax.rem(there, RUNS), plane, there // RUNS, core)
 
     def beside(k):
         return at(run, lax.rem(px + k // 4, 4) * 4 + lax.rem(py + k % 4, 4), group, core)
@@ -65,12 +60,12 @@
         pltpu.make_async_copy(ref, ref, send_sem.at[k]).wait()
 
     barrier = pltpu.get_barrier_semaphore()
-    greeted = [beside(k) for k in PLANE] + [ring(k) for k in (4, -4, 3, -3, 2, -2, 1, -1)] + [sibling]
+    greeted = [across(1), across(3)] + [along(k) for k in (2, 1, 3)] + [beside(k) for k in (8, 2, 4, 12, 1, 3)] + [sibling]
     for device in greeted:
         pl.semaphore_signal(barrier, inc=1, device_id=device, device_id_type=MESH)
     loads = [
-        pltpu.make_async_copy(query_hbm, query.at[plane], load_sem.at[0]),
-        pltpu.make_async_copy(hess_hbm, hess.at[run], load_sem.at[1]),
+        pltpu.make_async_copy(query_hbm, query.at[px, run], load_sem.at[0]),
+        pltpu.make_async_copy(hess_hbm, hess.at[py], load_sem.at[1]),
         pltpu.make_async_copy(proj_hbm, proj, load_sem.at[2]),
         pltpu.make_async_copy(acts_hbm, acts, load_sem.at[3]),
         pltpu.make_async_copy(grads_hbm, grads, load_sem.at[4]),
@@ -93,13 +88,11 @@
         load.wait()
 
     pl.semaphore_wait(barrier, len(greeted))
-    for k in (4, -4):
-        pl.semaphore_signal(known, inc=1, device_id=ring(k), device_id_type=MESH)
     send(rows.at[1 - core], pair, 0, sibling)
-    for k in PLANE:
-        send(query.at[plane], query.at[plane], 1, beside(k))
-    for k in (2, 1, 3):
-        send(hess.at[run], hess.at[run], 2, along(k))
+    for k in (2, 1, 3):
+        send(query.at[px, run], query.at[px, run], 1, along(k))
+    for k in (2, 1, 3):
+        send(hess.at[py], hess.at[py], 2, beside(k))
     arrived(pair, 0)
     chip = rows[core] + pair[...]
     halves = [chip[: HALF // 2], chip[HALF // 2 :]]
@@ -112,40 +105,32 @@
             send(codes.at[slot], codes_in.at[slot], 10 + slot, device)
             send(scales.at[slot], scales_in.at[slot], 14 + slot, device)
         if step == 0:
+            arrived(query.at[0, pl.ds(0, RUNS - 1)], 1)
+            for k in (8, 4, 12):
+                send(query.at[px], query.at[px], 3, beside(k))
             for half in range(2):
                 arrived(codes.at[half], 10 + half)
                 arrived(scales.at[half], 14 + half)
                 halves[half] = halves[half] + decode(codes_in[half], scales_in[half])
 
-    arrived(query.at[pl.ds(0, NEAR - 1)], 1)
-    arrived(hess.at[pl.ds(0, RUNS - 1)], 2)
+    arrived(query.at[pl.ds(0, 3)], 3)
+    arrived(hess.at[pl.ds(0, 3)], 2)
     contract = (((1,), (1,)), ((), ()))
-    rows_of_hess = hess[...].reshape(RUNS * RANK, 512)
+    rows_of_hess = hess[...].reshape(4 * RANK, 512)
 
     def times(which):
-        some = query[pl.ds(which * 8, 8)].reshape(HALF, 512)
-        result = lax.dot_general(rows_of_hess, some, contract, preferred_element_type=jnp.float32)
-        return result.reshape(RUNS, RANK, HALF)
+        some = query[pl.ds(which * 2, 2)].reshape(HALF, 512)
+        return lax.dot_general(some, rows_of_hess, contract, preferred_element_type=jnp.float32)
 
     product[...] = times(1 - core)
     send(product, others, 4, sibling)
     own = times(core)
     arrived(others, 4)
-    summed[...] = (own + others[...]).astype(jnp.bfloat16)
-    pl.semaphore_wait(known, 2)
+    both = (own + others[...]).astype(jnp.bfloat16).reshape(2, RUNS, 16, 4 * RANK)
     for k in range(RUNS):
-        stays = jnp.logical_and(group == run, run == k)
-
-        @pl.when(jnp.logical_not(stays))
-        def _():
-            pltpu.make_async_remote_copy(
-                summed.at[k], blocks.at[group], block_sem.at[k], recv_sem.at[5],
-                device_id=at(k, plane, run, core), device_id_type=MESH,
-            ).start()
-
-        @pl.when(stays)
-        def _():
-            pltpu.make_async_copy(summed.at[k], blocks.at[group], recv_sem.at[5]).start()
+        summed[k] = both[:, k]
+    for k in (2, 1, 3):
+        send(summed.at[lax.rem(group + k, RUNS)], blocks.at[k - 1], 5, across(k))
 
     for half in range(2):
         arrived(codes.at[2 + half], 12 + half)
@@ -160,31 +145,46 @@
     send(partial, partner, 6, sibling)
     arrived(partner, 6)
     rounded = (partial[...] + partner[...]).astype(jnp.bfloat16)
-    to = lax.broadcasted_iota(jnp.int32, (NEAR * 8, RANK), 0)
-    come = lax.broadcasted_iota(jnp.int32, (NEAR * 8, RANK), 1)
-    to_run, to_plane = lax.rem(to, 8), lax.div(to, 8)
-    chosen = jnp.logical_and(to_run < RUNS, come == to_run * NEAR + to_plane)
-    order = jnp.where(chosen, 1.0, 0.0).astype(jnp.bfloat16)
-    ordered = jnp.dot(order, rounded, preferred_element_type=jnp.float32)
-    factor[...] = ordered.reshape(NEAR, 8, 2 * RANK)
+    def iota(rows_, lanes, axis):
+        return lax.broadcasted_iota(jnp.int32, (rows_, lanes), axis)
+
+    def matrix(condition):
+        return jnp.where(condition, 1.0, 0.0).astype(jnp.bfloat16)
+
+    twice = matrix(iota(2 * RANK, 2 * RANK, 0) == lax.rem(iota(2 * RANK, 2 * RANK, 1), RANK))
+    doubled = jnp.dot(rounded, twice, preferred_element_type=jnp.float32)
+    parity = lax.rem(iota(RANK, 2 * RANK, 0), 2) == lax.div(iota(RANK, 2 * RANK, 1), RANK)
+    doubled = jnp.where(parity, doubled, 0.0).astype(jnp.bfloat16)
+    to, come = iota(32, RANK, 0), iota(32, RANK, 1)
+    order = matrix(
+        jnp.logical_and(
+            lax.div(to, 8) == lax.rem(lax.div(come, 4), 4),
+            lax.rem(to, 8) == lax.div(come, 16) * 2 + lax.div(lax.rem(come, 4), 2),
+        )
+    )
+    ordered = jnp.dot(order, doubled, preferred_element_type=jnp.float32)
+    factor[...] = ordered.reshape(4, 8, 2 * RANK)
     for k in PLANE:
-        there = lax.rem(px + k // 4, 4) * 4 + lax.rem(py + k % 4, 4)
-        send(factor.at[there], factors.at[plane], 7, beside(k))
-    factors[plane] = factor[plane]
+        send(factor.at[lax.rem(px + k // 4, 4)], factors.at[plane], 7, beside(k))
+    factors[plane] = factor[px]
 
     arrived(blocks, 5)
     b = blocks[...].astype(jnp.float32)
-    gathered[run] = (b[0] + b[1] + (b[2] + b[3])).astype(jnp.bfloat16)
+    gathered[run] = (summed[group].astype(jnp.float32) + b[0] + (b[1] + b[2])).astype(jnp.bfloat16)
     for k in (2, 1, 3):
         send(gathered.at[run], gathered.at[run], 8, along(k))
     arrived(factors.at[pl.ds(0, NEAR - 1)], 7)
-    left_side = factors[...].reshape(NEAR * 8, 2 * RANK)[:, :RANK].astype(jnp.bfloat16)
-    which = lax.rem(lax.broadcasted_iota(jnp.int32, (NEAR * 8, HALF), 0), 8)
+    left_side = factors[...].reshape(NEAR * 8, 2 * RANK).astype(jnp.bfloat16)
+    which = lax.rem(iota(NEAR * 8, HALF, 0), 8)
     arrived(gathered.at[pl.ds(0, RUNS - 1)], 8)
     scores = jnp.zeros((NEAR * 8, HALF), jnp.float32)
-    for k in range(RUNS):
-        term = jnp.dot(left_side, gathered[k], preferred_element_type=jnp.float32)
+    for k in range(2 * RUNS):
+        piece = gathered[k // 2, :, :, (k % 2) * 128 : (k % 2) * 128 + 128]
+        right_side = jnp.concatenate([piece[0]] * 4 + [piece[1]] * 4, axis=0)
+        term = lax.dot_general(left_side, right_side, contract, preferred_element_type=jnp.float32)
         scores += jnp.where(which == k, term, 0.0)
+    mine = lax.div(lax.rem(iota(NEAR * 8, HALF, 1), 64), 16) == py
+    scores = jnp.where(mine, scores, 0.0)
     part[...] = scores.reshape(NEAR, 8, HALF)
     for k in PLANE:
         there = lax.rem(px + k // 4, 4) * 4 + lax.rem(py + k % 4, 4)
@@ -192,8 +192,9 @@
     parts[plane] = part[plane]
 
     left(pair, 0)
-    left(query.at[pl.ds(0, NEAR - 1)], 1)
-    left(hess.at[pl.ds(0, RUNS - 1)], 2)
+    left(query.at[0, pl.ds(0, RUNS - 1)], 1)
+    left(hess.at[pl.ds(0, 3)], 2)
+    left(query.at[pl.ds(0, 3)], 3)
     for slot in range(4):
         left(codes.at[slot], 10 + slot)
         left(scales.at[slot], 14 + slot)
@@ -201,10 +202,7 @@
     left(partner, 6)
     left(factors.at[pl.ds(0, NEAR - 1)], 7)
     left(gathered.at[pl.ds(0, RUNS - 1)], 8)
-    for k in range(RUNS):
-        @pl.when(jnp.logical_not(jnp.logical_and(group == run, run == k)))
-        def _():
-            pltpu.make_async_copy(summed.at[k], summed.at[k], block_sem.at[k]).wait()
+    left(blocks, 5)
     arrived(parts.at[pl.ds(0, NEAR - 1)], 9)
     total = jnp.sum(parts[...], axis=0)
     out[...] = jnp.sum(total, axis=0, keepdims=True)
@@ -227,22 +225,20 @@
         pltpu.VMEM((4, 8, 128), f32),
         pltpu.VMEM((RANK, 128), f32),
         pltpu.VMEM((RANK, 128), f32),
+        pltpu.VMEM((4, 8, 128), f32),
         pltpu.VMEM((NEAR, 8, 128), f32),
-        pltpu.VMEM((NEAR, 8, 128), f32),
-        pltpu.VMEM((RUNS, RANK, 512), bf16),
-        pltpu.VMEM((NEAR, 16, 512), bf16),
-        pltpu.VMEM((RUNS, RANK, HALF), f32),
-        pltpu.VMEM((RUNS, RANK, HALF), f32),
-        pltpu.VMEM((RUNS, RANK, HALF), bf16),
-        pltpu.VMEM((RUNS, RANK, HALF), bf16),
-        pltpu.VMEM((RUNS, RANK, HALF), bf16),
+        pltpu.VMEM((4, RANK, 512), bf16),
+        pltpu.VMEM((4, RUNS, 16, 512), bf16),
+        pltpu.VMEM((HALF, 4 * RANK), f32),
+        pltpu.VMEM((HALF, 4 * RANK), f32),
+        pltpu.VMEM((RUNS, 2, 16, 4 * RANK), bf16),
+        pltpu.VMEM((RUNS - 1, 2, 16, 4 * RANK), bf16),
+        pltpu.VMEM((RUNS, 2, 16, 4 * RANK), bf16),
         pltpu.VMEM((NEAR, 8, HALF), f32),
         pltpu.VMEM((NEAR, 8, HALF), f32),
         pltpu.SemaphoreType.DMA((6,)),
         pltpu.SemaphoreType.DMA((18,)),
         pltpu.SemaphoreType.DMA((18,)),
-        pltpu.SemaphoreType.DMA((RUNS,)),
-        pltpu.SemaphoreType.REGULAR,
     ]
     return pl.pallas_call(
         attribute,

time: 44 us -> 41.9 us (0.952)
  Pallas kernels: 41.8 us -> 39.9 us
    pallas_call x1, Pallas kernels: 41.8 us -> 39.9 us  [on_device(): pl.pallas_call(attribute, out_shape=jax.ShapeDtypeStruct((1, HALF), f32),...]
where the time goes in v3:
time: 41.9 us; the launch traced here: 41.8 us
  Pallas kernels  39.9 us (95%)
  local copies, waits for them, and re-layouts  1.19 us (3%)
  between operations  0.66 us (2%)
    pallas_call x1, Pallas kernels, on_device(): pl.pallas_call(attribute, out_shape=jax.ShapeDtypeStruct((1, HALF), f32),...  39.9 us
    unnamed x1, local copies, waits for them, and re-layouts  1.19 us

profile of v3, /device:TPU:1, one launch (start us, length us, event | category | flops | bytes accessed | tf_op | source)
XLA Modules:
  0.0 41.8 jit_solution(8965159586901422180)
XLA Ops:
  0.7 39.9 %attribute.1 = f32[1,128]{1,0:T(1,128)} custom-call(bf16[1,256,1024]{2,1,0:T(8,128)(2,1)} %acts_hbm.1, bf16[1,256,1024]{2,1,0:T(8,128)(2,1)} %grads_hbm.1, bf16[1024,128]{1,0:T(8,128)(2,1)} %proj_hbm.1, s32[1]{0:T(128)S(6)} %copy.8.counts_hbm, bf16[64,512]{1,0:T(8,128)(2,1)} %hess_hbm.1, bf16[16,512]{1,0:T(8,128)(2,1)} %query_hbm.1), custom_call_target="tpu_custom_call" | custom-call | flops 200000000 | bytes 1500000 | tf_op jit(solution)/shard_map/attribute/pallas_call | solution.py:243
  40.6 1.2 %copy.9 = f32[1,128]{1,0:T(1,128)} copy(f32[1,128]{1,0:T(1,128)} %attribute.1) | data formatting | bytes 1024

commit v4 on v3

--- a/solution.py
+++ b/solution.py
@@ -27,7 +27,7 @@
     acts_hbm, grads_hbm, proj_hbm, counts_hbm, hess_hbm, query_hbm, out,
     acts, grads, proj, counts, rows, pair, codes, codes_in, scales, scales_in, partial, partner, factor, factors,
     hess, query, product, others, summed, blocks, gathered, part, parts,
-    load_sem, send_sem, recv_sem,
+    load_sem, send_sem, recv_sem, piece_sem,
 ):
     d, s = lax.axis_index("dp"), lax.axis_index("tensor")
     run, plane = d // NEAR, lax.rem(d, NEAR)
@@ -89,14 +89,19 @@
 
     pl.semaphore_wait(barrier, len(greeted))
     send(rows.at[1 - core], pair, 0, sibling)
-    for k in (2, 1, 3):
-        send(query.at[px, run], query.at[px, run], 1, along(k))
+    for k in (1, 2, 3):
+        pltpu.make_async_remote_copy(
+            query.at[px, run], query.at[px, run], send_sem.at[1], piece_sem.at[RUNS - k - 1],
+            device_id=along(k), device_id_type=MESH,
+        ).start()
+    for k in (8, 4, 12):
+        send(query.at[px, run], query.at[px, run], 3, beside(k))
     for k in (2, 1, 3):
         send(hess.at[py], hess.at[py], 2, beside(k))
     arrived(pair, 0)
     chip = rows[core] + pair[...]
     halves = [chip[: HALF // 2], chip[HALF // 2 :]]
-    for step in range(2):
+    def exchange(step):
         for half in range(2):
             slot = 2 * step + half
             codes[slot], scales[slot] = encode(halves[half])
@@ -104,14 +109,21 @@
             device = at(run, plane, partner_group, core)
             send(codes.at[slot], codes_in.at[slot], 10 + slot, device)
             send(scales.at[slot], scales_in.at[slot], 14 + slot, device)
-        if step == 0:
-            arrived(query.at[0, pl.ds(0, RUNS - 1)], 1)
-            for k in (8, 4, 12):
-                send(query.at[px], query.at[px], 3, beside(k))
-            for half in range(2):
-                arrived(codes.at[half], 10 + half)
-                arrived(scales.at[half], 14 + half)
-                halves[half] = halves[half] + decode(codes_in[half], scales_in[half])
+
+    exchange(0)
+    first = jnp.where(run == 3, 3, 1)
+    second = jnp.where(jnp.logical_or(run == 0, run == 3), 2, 3)
+    for k in (first, second, 6 - first - second):
+        there = lax.rem(run + k, RUNS)
+        pltpu.make_async_copy(query.at[px, there], query.at[px, there], piece_sem.at[k - 1]).wait()
+        for j in (8, 4, 12):
+            send(query.at[px, there], query.at[px, there], 3, beside(j))
+
+    for half in range(2):
+        arrived(codes.at[half], 10 + half)
+        arrived(scales.at[half], 14 + half)
+        halves[half] = halves[half] + decode(codes_in[half], scales_in[half])
+    exchange(1)
 
     arrived(query.at[pl.ds(0, 3)], 3)
     arrived(hess.at[pl.ds(0, 3)], 2)
@@ -239,6 +251,7 @@
         pltpu.SemaphoreType.DMA((6,)),
         pltpu.SemaphoreType.DMA((18,)),
         pltpu.SemaphoreType.DMA((18,)),
+        pltpu.SemaphoreType.DMA((RUNS - 1,)),
     ]
     return pl.pallas_call(
         attribute,

time: 41.9 us -> 41.4 us (0.988)
  Pallas kernels: 39.9 us -> 39.1 us
    pallas_call x1, Pallas kernels: 39.9 us -> 39.1 us  [on_device(): pl.pallas_call(attribute, out_shape=jax.ShapeDtypeStruct((1, HALF), f32),...]
where the time goes in v4:
time: 41.4 us; the launch traced here: 40.9 us
  Pallas kernels  39.1 us (94%)
  local copies, waits for them, and re-layouts  1.19 us (3%)
  between operations  0.66 us (2%)
    pallas_call x1, Pallas kernels, on_device(): pl.pallas_call(attribute, out_shape=jax.ShapeDtypeStruct((1, HALF), f32),...  39.1 us
    unnamed x1, local copies, waits for them, and re-layouts  1.19 us

profile of v4, /device:TPU:1, one launch (start us, length us, event | category | flops | bytes accessed | tf_op | source)
XLA Modules:
  0.0 40.9 jit_solution(8515487567123867792)
XLA Ops:
  0.7 39.1 %attribute.1 = f32[1,128]{1,0:T(1,128)} custom-call(bf16[1,256,1024]{2,1,0:T(8,128)(2,1)} %acts_hbm.1, bf16[1,256,1024]{2,1,0:T(8,128)(2,1)} %grads_hbm.1, bf16[1024,128]{1,0:T(8,128)(2,1)} %proj_hbm.1, s32[1]{0:T(128)S(6)} %copy.8.counts_hbm, bf16[64,512]{1,0:T(8,128)(2,1)} %hess_hbm.1, bf16[16,512]{1,0:T(8,128)(2,1)} %query_hbm.1), custom_call_target="tpu_custom_call" | custom-call | flops 200000000 | bytes 1500000 | tf_op jit(solution)/shard_map/attribute/pallas_call | solution.py:256
  39.7 1.2 %copy.9 = f32[1,128]{1,0:T(1,128)} copy(f32[1,128]{1,0:T(1,128)} %attribute.1) | data formatting | bytes 1024

commit v5 on v4

--- a/solution.py
+++ b/solution.py
@@ -26,8 +26,8 @@
 def attribute(
     acts_hbm, grads_hbm, proj_hbm, counts_hbm, hess_hbm, query_hbm, out,
     acts, grads, proj, counts, rows, pair, codes, codes_in, scales, scales_in, partial, partner, factor, factors,
-    hess, query, product, others, summed, blocks, gathered, part, parts,
-    load_sem, send_sem, recv_sem, piece_sem,
+    hess, query, product, others, ours, summed, blocks, gathered, part, parts,
+    load_sem, send_sem, recv_sem, piece_sem, pair_sem,
 ):
     d, s = lax.axis_index("dp"), lax.axis_index("tensor")
     run, plane = d // NEAR, lax.rem(d, NEAR)
@@ -134,15 +134,26 @@
         some = query[pl.ds(which * 2, 2)].reshape(HALF, 512)
         return lax.dot_general(some, rows_of_hess, contract, preferred_element_type=jnp.float32)
 
-    product[...] = times(1 - core)
-    send(product, others, 4, sibling)
-    own = times(core)
-    arrived(others, 4)
-    both = (own + others[...]).astype(jnp.bfloat16).reshape(2, RUNS, 16, 4 * RANK)
+    def by_run(which):
+        return times(which).reshape(2, RUNS, 16, 4 * RANK)
+
+    away = [lax.rem(group + k, RUNS) for k in (2, 1, 3, 0)]
+    theirs = by_run(1 - core)
     for k in range(RUNS):
-        summed[k] = both[:, k]
-    for k in (2, 1, 3):
-        send(summed.at[lax.rem(group + k, RUNS)], blocks.at[k - 1], 5, across(k))
+        product[k] = theirs[:, k]
+    for k in away:
+        pltpu.make_async_remote_copy(
+            product.at[k], others.at[k], send_sem.at[4], pair_sem.at[k], device_id=sibling, device_id_type=MESH
+        ).start()
+    own = by_run(core)
+    for k in range(RUNS):
+        ours[k] = own[:, k]
+    for place, k in enumerate(away):
+        pltpu.make_async_copy(others.at[k], others.at[k], pair_sem.at[k]).wait()
+        summed[k] = (ours[k] + others[k]).astype(jnp.bfloat16)
+        if place < RUNS - 1:
+            apart = (2, 1, 3)[place]
+            send(summed.at[k], blocks.at[apart - 1], 5, across(apart))
 
     for half in range(2):
         arrived(codes.at[2 + half], 12 + half)
@@ -241,8 +252,9 @@
         pltpu.VMEM((NEAR, 8, 128), f32),
         pltpu.VMEM((4, RANK, 512), bf16),
         pltpu.VMEM((4, RUNS, 16, 512), bf16),
-        pltpu.VMEM((HALF, 4 * RANK), f32),
-        pltpu.VMEM((HALF, 4 * RANK), f32),
+        pltpu.VMEM((RUNS, 2, 16, 4 * RANK), f32),
+        pltpu.VMEM((RUNS, 2, 16, 4 * RANK), f32),
+        pltpu.VMEM((RUNS, 2, 16, 4 * RANK), f32),
         pltpu.VMEM((RUNS, 2, 16, 4 * RANK), bf16),
         pltpu.VMEM((RUNS - 1, 2, 16, 4 * RANK), bf16),
         pltpu.VMEM((RUNS, 2, 16, 4 * RANK), bf16),
@@ -252,6 +264,7 @@
         pltpu.SemaphoreType.DMA((18,)),
         pltpu.SemaphoreType.DMA((18,)),
         pltpu.SemaphoreType.DMA((RUNS - 1,)),
+        pltpu.SemaphoreType.DMA((RUNS,)),
     ]
     return pl.pallas_call(
         attribute,

time: 41.4 us -> 41.1 us (level)
  no operation moved by 1% of the time
where the time goes in v5:
time: 41.1 us; the launch traced here: 40.9 us
  Pallas kernels  39.1 us (95%)
  local copies, waits for them, and re-layouts  1.19 us (3%)
  between operations  0.66 us (2%)
    pallas_call x1, Pallas kernels, on_device(): pl.pallas_call(attribute, out_shape=jax.ShapeDtypeStruct((1, HALF), f32),...  39.1 us
    unnamed x1, local copies, waits for them, and re-layouts  1.19 us

profile of v5, /device:TPU:1, one launch (start us, length us, event | category | flops | bytes accessed | tf_op | source)
XLA Modules:
  0.0 40.9 jit_solution(9855597010832964018)
XLA Ops:
  0.7 39.1 %attribute.1 = f32[1,128]{1,0:T(1,128)} custom-call(bf16[1,256,1024]{2,1,0:T(8,128)(2,1)} %acts_hbm.1, bf16[1,256,1024]{2,1,0:T(8,128)(2,1)} %grads_hbm.1, bf16[1024,128]{1,0:T(8,128)(2,1)} %proj_hbm.1, s32[1]{0:T(128)S(6)} %copy.8.counts_hbm, bf16[64,512]{1,0:T(8,128)(2,1)} %hess_hbm.1, bf16[16,512]{1,0:T(8,128)(2,1)} %query_hbm.1), custom_call_target="tpu_custom_call" | custom-call | flops 200000000 | bytes 1500000 | tf_op jit(solution)/shard_map/attribute/pallas_call | solution.py:269
  39.7 1.2 %copy.9 = f32[1,128]{1,0:T(1,128)} copy(f32[1,128]{1,0:T(1,128)} %attribute.1) | data formatting | bytes 1024

commit v6 on v5

--- a/solution.py
+++ b/solution.py
@@ -208,7 +208,7 @@
         scores += jnp.where(which == k, term, 0.0)
     mine = lax.div(lax.rem(iota(NEAR * 8, HALF, 1), 64), 16) == py
     scores = jnp.where(mine, scores, 0.0)
-    part[...] = scores.reshape(NEAR, 8, HALF)
+    part[...] = jnp.sum(scores.reshape(NEAR, 8, HALF), axis=1, keepdims=True)
     for k in PLANE:
         there = lax.rem(px + k // 4, 4) * 4 + lax.rem(py + k % 4, 4)
         send(part.at[there], parts.at[plane], 9, beside(k))
@@ -227,8 +227,7 @@
     left(gathered.at[pl.ds(0, RUNS - 1)], 8)
     left(blocks, 5)
     arrived(parts.at[pl.ds(0, NEAR - 1)], 9)
-    total = jnp.sum(parts[...], axis=0)
-    out[...] = jnp.sum(total, axis=0, keepdims=True)
+    out[...] = jnp.sum(parts[...], axis=0)
     left(parts.at[pl.ds(0, NEAR - 1)], 9)
 
 
@@ -258,8 +257,8 @@
         pltpu.VMEM((RUNS, 2, 16, 4 * RANK), bf16),
         pltpu.VMEM((RUNS - 1, 2, 16, 4 * RANK), bf16),
         pltpu.VMEM((RUNS, 2, 16, 4 * RANK), bf16),
-        pltpu.VMEM((NEAR, 8, HALF), f32),
-        pltpu.VMEM((NEAR, 8, HALF), f32),
+        pltpu.VMEM((NEAR, 1, HALF), f32),
+        pltpu.VMEM((NEAR, 1, HALF), f32),
         pltpu.SemaphoreType.DMA((6,)),
         pltpu.SemaphoreType.DMA((18,)),
         pltpu.SemaphoreType.DMA((18,)),

time: 41.1 us -> 41 us (level)
  no operation moved by 1% of the time
where the time goes in v6:
time: 41 us; the launch traced here: 40.8 us
  Pallas kernels  39 us (95%)
  local copies, waits for them, and re-layouts  1.19 us (3%)
  between operations  0.66 us (2%)
    pallas_call x1, Pallas kernels, on_device(): pl.pallas_call(attribute, out_shape=jax.ShapeDtypeStruct((1, HALF), f32),...  39 us
    unnamed x1, local copies, waits for them, and re-layouts  1.19 us

profile of v6, /device:TPU:1, one launch (start us, length us, event | category | flops | bytes accessed | tf_op | source)
XLA Modules:
  0.0 40.8 jit_solution(12036703855427171796)
XLA Ops:
  0.7 39.0 %attribute.1 = f32[1,128]{1,0:T(1,128)} custom-call(bf16[1,256,1024]{2,1,0:T(8,128)(2,1)} %acts_hbm.1, bf16[1,256,1024]{2,1,0:T(8,128)(2,1)} %grads_hbm.1, bf16[1024,128]{1,0:T(8,128)(2,1)} %proj_hbm.1, s32[1]{0:T(128)S(6)} %copy.8.counts_hbm, bf16[64,512]{1,0:T(8,128)(2,1)} %hess_hbm.1, bf16[16,512]{1,0:T(8,128)(2,1)} %query_hbm.1), custom_call_target="tpu_custom_call" | custom-call | flops 200000000 | bytes 1500000 | tf_op jit(solution)/shard_map/attribute/pallas_call | solution.py:268
  39.7 1.2 %copy.9 = f32[1,128]{1,0:T(1,128)} copy(f32[1,128]{1,0:T(1,128)} %attribute.1) | data formatting | bytes 1024
